TPU v7x, 512 devices: a whole 4x8x8 slice. The times are simulated.
512 devices in a mesh: mp: 8 (over z_hi, core), ctx: 64 (over z_lo, x, y).
Axes of the slice: x: 4, y: 8, z: 8 (z_hi: 4, z_lo: 2; z = z_hi * 2 + z_lo), core: 2. Of those that a mesh axis runs over, the one named last changes fastest.
Arguments:
- x_in: bfloat16 [16384, 8192], P('ctx', 'mp'), may hold values from -6 to 6
- z_gate: bfloat16 [16384, 8192], P('ctx', 'mp'), may hold values from -6 to 6
- dt_raw: bfloat16 [16384, 8192], P('ctx', 'mp'), may hold values from -6 to 6
- b_proj: bfloat16 [16384, 16], P('ctx'), may hold values from -0.6 to 0.6
- c_proj: bfloat16 [16384, 16], P('ctx'), may hold values from -1.796875 to 1.796875
- conv_weight: float32 [4, 8192], P(None, 'mp'), may hold values from -3 to 3
- conv_bias: float32 [8192], P('mp'), may hold values from -3 to 3
- a_log: float32 [16, 8192], P(None, 'mp'), may hold values from -11.4 to -2.8, as said below
- d_skip: float32 [8192], P('mp'), may hold values from 0.5 to 1.5
Outputs:
- mamba_out: bfloat16 [16384, 8192], P('ctx', 'mp')
Inputs may be any that keep to these rules, and one draw needn't show every extreme that they name: a_log holds logarithms of positive decay rates.
All inputs are finite; a program needn't handle non-finite values.
Results may differ from a plain program's by a relative error of at most 0.0014.
Values may be sent and summed in bfloat16 or wider, within the bound.
A program may use at most 64 MiB of HBM per device.

v0:
```python
import jax
import jax.numpy as jnp
from jax import lax
from jax.sharding import PartitionSpec as P


def from_behind(value, axis, steps):
    count = lax.axis_size(axis)
    first, last = (max(0, -steps), min(count, count - steps))
    return lax.ppermute(value, axis, [(source, source + steps) for source in range(first, last)])


def prefix(part, axis, combine, identity):
    place = lax.axis_index(axis)
    gathered = jax.tree.map(lambda a: lax.all_gather(a, axis), part)
    state = jax.tree.map(lambda a, e: jnp.zeros_like(a) + jnp.asarray(e, a.dtype), part, identity)

    def one(turn, state):
        return combine(
            state, jax.tree.map(lambda a: lax.dynamic_index_in_dim(a, turn, 0, False), gathered)
        )

    return lax.fori_loop(0, place, one, state)


def combine_pair(earlier, later):
    return (earlier[0] * later[0], later[0] * earlier[1] + later[1])


def in_blocks(array, span_len):
    return array.reshape((array.shape[0] // span_len, span_len) + array.shape[1:])


def body(x_in, z_gate, dt_raw, b_proj, c_proj, conv_weight, conv_bias, a_log, d_skip):
    row_count, channels = x_in.shape
    conv_taps = conv_weight.shape[0]
    prior_rows = from_behind(x_in[row_count - (conv_taps - 1) :], "ctx", 1)
    prior_f = prior_rows.astype(jnp.float32)
    x_values = x_in.astype(jnp.float32)
    conv_sum = conv_bias[None, :] + conv_weight[conv_taps - 1][None, :] * x_values
    for back in range(1, conv_taps):
        tap = conv_weight[conv_taps - 1 - back][None, :]
        conv_sum = conv_sum.at[back:].add(tap * x_values[: row_count - back])
        conv_sum = conv_sum.at[:back].add(tap * prior_f[conv_taps - 1 - back :])
    inner_act = jax.nn.silu(conv_sum)
    step_size = jax.nn.softplus(dt_raw.astype(jnp.float32))
    rates = -jnp.exp(a_log)
    b_values = b_proj.astype(jnp.float32)
    c_values = c_proj.astype(jnp.float32)
    gate_act = jax.nn.silu(z_gate.astype(jnp.float32))
    span_len = 16

    def local_pass(carried, blk):
        ssm_state, running = carried
        inner_blk, step_blk, drive_blk, read_blk = blk
        mixed_rows = []
        sum_rows = []
        for inside in range(span_len):
            step_row = step_blk[inside]
            ssm_state = (
                jnp.exp(step_row[None, :] * rates) * ssm_state
                + (step_row * inner_blk[inside])[None, :] * drive_blk[inside][:, None]
            )
            mixed_rows.append(
                jnp.sum(read_blk[inside][:, None] * ssm_state, axis=0) + d_skip * inner_blk[inside]
            )
            running = running + step_row
            sum_rows.append(running)
        return ((ssm_state, running), (jnp.stack(mixed_rows), jnp.stack(sum_rows)))

    zero_state = jnp.zeros((a_log.shape[0], channels), jnp.float32)
    zero_sum = jnp.zeros((channels,), jnp.float32)
    pieces = (
        in_blocks(inner_act, span_len),
        in_blocks(step_size, span_len),
        in_blocks(b_values, span_len),
        in_blocks(c_values, span_len),
    )
    (end_state, step_total), (local_blocks, cum_blocks) = lax.scan(
        local_pass, (zero_state, zero_sum), pieces
    )
    local_mixed = local_blocks.reshape(row_count, channels)
    carried = prefix(
        (jnp.exp(rates * step_total[None, :]), end_state),
        "ctx",
        combine_pair,
        (jnp.ones_like(end_state), zero_state),
    )
    start_state = carried[1]

    def carry_readout(blk):
        cum_blk, read_blk = blk
        decayed = jnp.exp(cum_blk[:, None, :] * rates[None]) * start_state[None]
        return jnp.sum(read_blk[:, :, None] * decayed, axis=1)

    carried_blocks = lax.map(carry_readout, (cum_blocks, in_blocks(c_values, span_len)))
    mixed_all = local_mixed + carried_blocks.reshape(row_count, channels)
    return (mixed_all * gate_act).astype(jnp.bfloat16)


def solution(mesh):
    in_specs = (
        P("ctx", "mp"),
        P("ctx", "mp"),
        P("ctx", "mp"),
        P("ctx", None),
        P("ctx", None),
        P(None, "mp"),
        P("mp"),
        P(None, "mp"),
        P("mp"),
    )
    out_specs = P("ctx", "mp")
    return jax.shard_map(body, mesh=mesh, in_specs=in_specs, out_specs=out_specs, check_vma=False)
```

profile of v0, /device:TPU:126, one launch (start us, length us, event | category | flops | bytes accessed | tf_op | source)
XLA Modules:
  0.0 983.6 jit_solution(9551354079941020280)
XLA Ops:
  10.6 2.6 compare_select_fusion
  19.9 260.5 %while.47 = (s32[]{:T(128)}, f32[16,1024]{1,0:T(8,128)S(1)}, f32[1024]{0:T(1024)}, f32[16,16,1024]{2,1,0:T(8,128)S(1)}, f32[16,16,1024]{2,1,0:T(8,128)S(1)}, /*i...) while((s32[]{:T(128)}, f32[16,1024]{1,0:T(8,128)S(1)}, ...), condition=%wide.region_17.18_spmd.clone, body=%wide.region_0.17_spmd.clone.sunk | while | flops 2376722 | bytes 2907717 | solution.py:79
  21.6 1.7 fusion.73
  35.5 1.7 fusion.72
  37.2 1.8 fusion.73
  52.0 1.7 fusion.72
  53.7 1.7 fusion.73
  70.2 1.7 fusion.73
  84.8 1.7 fusion.72
  86.5 1.7 fusion.73
  101.1 1.7 fusion.72
  102.8 1.7 fusion.73
  119.1 1.7 fusion.73
  133.7 1.7 fusion.72
  135.4 1.7 fusion.73
  151.7 1.7 fusion.73
  166.3 1.7 fusion.72
  168.0 1.7 fusion.73
  182.6 1.7 fusion.72
  184.3 1.7 fusion.73
  200.6 1.7 fusion.73
  215.2 1.7 fusion.72
  216.9 1.7 fusion.73
  233.1 1.7 fusion.73
  249.4 1.7 fusion.73
  264.0 1.7 fusion.72
  265.7 1.7 fusion.73
  282.6 308.5 %all-gather.7.cloned.1.call-done = f32[1024,1024]{1,0:T(8,128)} async-done(((f32[16,1024]{1,0:T(8,128)}), f32[1024,1024]{1,0:T(8,128)}) %all-gather.7.cloned.1.call-update) | async-done | bytes 4194320 | tf_op jit(solution)/shard_map/all_gather | solution.py:15
  591.1 306.2 %all-gather.5.cloned.1.call-done = f32[1024,1024]{1,0:T(8,128)} async-done(((f32[16,1024]{1,0:T(8,128)}), f32[1024,1024]{1,0:T(8,128)}) %all-gather.5.cloned.1.call-update) | async-done | bytes 4194320 | tf_op jit(solution)/shard_map/all_gather | solution.py:15
  897.3 58.3 %while.45 = (s32[]{:T(128)}, f32[16,1024]{1,0:T(8,128)S(1)}, s32[]{:T(128)}, f32[64,16,1024]{2,1,0:T(8,128)}, f32[64,16,1024]{2,1,0:T(8,128)}, /*index=5*/s32[]{:T(128)}, s32[]{:T(128)}, s32[]{:T(128)}) while((s32[]{:T(128)}, f32[16,1024]{1,0:T(8,128)S(1)}, s32[]{:T(128)}, f32[64,16,1024]{2,1,0:T(8,128)}, f32[64,16,1024]{2,1,0:T(8,128)}, ...), condition=%wide.region_19.20_spmd, body=%wide.region_18.19_spmd.sunk | while | flops 32773 | bytes 262275 | solution.py:23
  955.7 18.8 %while.46 = (s32[]{:T(128)}, f32[16,16,1024]{2,1,0:T(8,128)S(1)}, f32[16,16,16]{2,1,0:T(8,128)}, f32[16,16,1024]{2,1,0:T(8,128)S(1)}, f32[16,1024]{1,0:T(8,128)S(1)}, /*index=5*/f32[16,1024]{1,0:T(8,128)S(1)}, s32[]{:T(128)}) while((s32[]{:T(128)}, f32[16,16,1024]{2,1,0:T(8,128)S(1)}, f32[16,16,16]{2,1,0:T(8,128)}, ...), condition=%wide.region_22.23_spmd, body=%wide.region_20.22_spmd.sunk | while | flops 1032194 | bytes 527457 | solution.py:96
  974.6 2.2 fusion.60
  (866 shorter events, 302.4 us)
Async XLA Ops:
  6.5 8.1 copy-start.8
  6.5 8.1 copy-start.10
  6.5 8.9 copy-start.11
  6.5 584.6 %all-gather.7.cloned.1.call-start = ((), (), s32[]{:S(2)}) async-start(), calls=%async_computation.1 | async-start | bytes 4259840 | tf_op jit(solution)/shard_map/all_gather | solution.py:15
  7.3 9.6 collective-permute-start
  10.6 6.4 copy-start.9
  39.2 5.8 copy-start.4
  39.2 5.8 copy-start.7
  55.6 6.0 copy-start.4
  55.6 6.0 copy-start.7
  72.1 5.8 copy-start.4
  72.1 5.8 copy-start.7
  88.4 5.8 copy-start.4
  104.7 5.9 copy-start.4
  104.7 5.9 copy-start.7
  121.0 5.8 copy-start.4
  137.3 5.8 copy-start.4
  153.6 5.8 copy-start.4
  153.6 5.8 copy-start.7
  169.9 5.8 copy-start.4
  169.9 5.8 copy-start.7
  186.2 5.8 copy-start.4
  186.2 5.8 copy-start.7
  202.4 5.8 copy-start.4
  202.5 5.8 copy-start.7
  218.7 5.8 copy-start.4
  235.0 5.8 copy-start.4
  251.3 5.8 copy-start.4
  251.3 5.8 copy-start.7
  267.6 5.9 copy-start.4
  267.6 5.9 copy-start.7
  281.0 616.3 %all-gather.5.cloned.1.call-start = ((), (), s32[]{:S(2)}) async-start(), calls=%async_computation | async-start | bytes 4259840 | tf_op jit(solution)/shard_map/all_gather | solution.py:15
  (88 other events, 198.8 us)
Sparse Core Ops, SparseCore 0:
  281.2 309.9 all-gather.6
  593.2 304.0 all-gather.4
where the time goes:
time: 995 us; the launch traced here: 984 us
  waiting for transfers between devices  615 us (62%)
  other arithmetic  236 us (24%)
  local copies, waits for them, and re-layouts  112 us (11%)
  between operations  13.7 us (1%)
    all_gather x2, waiting for transfers between devices, prefix(): gathered = jax.tree.map(lambda a: lax.all_gather(a, axis), part)  615 us
    reduce_sum x80, other arithmetic, local_pass(): jnp.sum(read_blk[inside][:, None] * ssm_state, axis=0)  70.4 us
    add x63, other arithmetic, combine_pair(): return (earlier[0] * later[0], later[0] * earlier[1] + later[1])  57.1 us
    mul x240, other arithmetic, local_pass(): step_row * inner_blk[inside]  48.2 us
    mul x16, local copies, waits for them, and re-layouts, local_pass(): (step_row * inner_blk[inside])[None, :] * drive_blk[inside][:, None]  27.4 us
    mul x16, local copies, waits for them, and re-layouts, local_pass(): read_blk[inside][:, None] * ssm_state  27 us
    add x32, other arithmetic, local_pass(): jnp.sum(read_blk[inside][:, None] * ssm_state, axis=0)  24.2 us
    slice x16, local copies, waits for them, and re-layouts, local_pass(): step_row = step_blk[inside]  21.9 us
  transfers between devices with their start and end apart: 3, of which 2 were waited for; matrix products, arithmetic and copies ran while one was open for 1% of the time, Pallas kernels for 0%

commit v1 on v0

v1 whole, which is shorter than its diff:
```python
import functools

import jax
import jax.numpy as jnp
from jax import lax
from jax.experimental import pallas as pl
from jax.experimental.pallas import tpu as pltpu
from jax.sharding import PartitionSpec as P

MESH = pl.DeviceIdType.MESH
F32 = jnp.float32
LANES = 128
SUB = 8
LINE = 8
HEAD = 4
LOG2E = 1.4426950408889634
LN2 = 0.6931471805599453
SHARES = ((0, 1, 2, 3, 4, 5), (6, 7, 8, 9, 10, 11), (12, 13, 14, 15))


def tile(index, count=1):
    if isinstance(index, int):
        return pl.ds(index * SUB, count * SUB)
    return pl.ds(pl.multiple_of(index * SUB, SUB), count * SUB)


def splat(ref, index):
    return ref[pl.ds(index, SUB, stride=0), :]


def kernel(lines, x_hbm, z_hbm, dt_hbm, b_hbm, c_hbm, w_hbm, bias_hbm, a_hbm, skip_hbm, out_ref,
           x_in, z_in, dt_in, b_in, c_in, w_in, bias_in, a_in, skip_in,
           x_rows, dt_rows, u_rows, sum_rows, y_rows, gate, b_splat, c_splat, rates, taps, decayed, ends,
           halo, parts_out, parts_in, total_out, total_in, carry, spans, starts_out, starts,
           load_sem, halo_sem, send1, recv1, send2, recv2, send3, recv3):
    tokens, channels = x_in.shape
    states = a_in.shape[0]
    per = states // LINE
    groups = channels // LANES
    me = lax.axis_index("ctx")
    line, place = me // LINE, me % LINE
    count = lines * LINE

    pairs = ((dt_hbm, dt_in), (a_hbm, a_in), (b_hbm, b_in), (x_hbm, x_in), (w_hbm, w_in),
             (bias_hbm, bias_in), (skip_hbm, skip_in), (c_hbm, c_in), (z_hbm, z_in))
    loads = [pltpu.make_async_copy(src, dst, load_sem.at[i]) for i, (src, dst) in enumerate(pairs)]
    for load in loads:
        load.start()
    dt_load, a_load, b_load, x_load, w_load, bias_load, skip_load, c_load, z_load = loads

    def in_line(step):
        return line * LINE + (place + step) % LINE

    barrier = pltpu.get_barrier_semaphore()
    for step in range(1, LINE):
        pl.semaphore_signal(barrier, inc=1, device_id={"ctx": in_line(step)}, device_id_type=MESH)
    for other in range(lines):
        @pl.when(other != line)
        def _():
            pl.semaphore_signal(barrier, inc=1, device_id={"ctx": other * LINE + place}, device_id_type=MESH)

    @pl.when(me > 0)
    def _():
        pl.semaphore_signal(barrier, inc=1, device_id={"ctx": me - 1}, device_id_type=MESH)

    def copy_to(src, dst, send, recv, target):
        return pltpu.make_async_remote_copy(src_ref=src, dst_ref=dst, send_sem=send, recv_sem=recv,
                                            device_id={"ctx": target}, device_id_type=MESH)

    halo_copy = copy_to(x_rows.at[pl.ds((tokens - 3) * SUB, 3 * SUB)], halo, halo_sem.at[0], halo_sem.at[1], me + 1)

    zero = jnp.zeros((SUB, LANES), F32)
    one = jnp.ones((SUB, LANES), F32)

    dt_load.wait()

    def step_sizes(i, _):
        rows = pl.ds(pl.multiple_of(i * 16, 16), 16)
        for j in range(groups):
            raw = dt_in[rows, j * LANES:(j + 1) * LANES].astype(F32)
            dt_rows[pl.ds(i * 16 * SUB + j, 16, stride=SUB), :] = jnp.log2(1.0 + jnp.exp2(raw * LOG2E))
        return 0

    lax.fori_loop(0, tokens // 16, step_sizes, 0)

    a_load.wait()
    for j in range(groups):
        rates[pl.ds(j, states, stride=SUB), :] = -jnp.exp(a_in[:, j * LANES:(j + 1) * LANES])

    def spread(src, dst):
        wide = 2 * LANES
        for n in range(0, states, 2):
            state_of = lax.broadcasted_iota(jnp.int32, (states, wide), 0)
            lane = lax.broadcasted_iota(jnp.int32, (states, wide), 1)
            pick = jnp.where(state_of == n + lane // LANES, 1.0, 0.0).astype(jnp.bfloat16)
            both = lax.dot_general(src[...], pick, (((0,), (0,)), ((), ())), preferred_element_type=F32)
            dst[n * tokens:(n + 1) * tokens, :] = both[:, :LANES]
            dst[(n + 1) * tokens:(n + 2) * tokens, :] = both[:, LANES:]

    b_load.wait()
    spread(b_in, b_splat)

    x_load.wait()

    def lay_out(i, _):
        rows = pl.ds(pl.multiple_of(i * 16, 16), 16)
        for j in range(groups):
            x_rows[pl.ds(i * 16 * SUB + j, 16, stride=SUB), :] = x_in[rows, j * LANES:(j + 1) * LANES].astype(F32)
        return 0

    lax.fori_loop(0, tokens // 16, lay_out, 0)
    w_load.wait()
    bias_load.wait()
    skip_load.wait()
    for j in range(groups):
        taps[pl.ds(j, 4, stride=SUB), :] = 0.5 * w_in[:, j * LANES:(j + 1) * LANES]
    tap = [taps[tile(k), :] for k in range(4)]
    bias = 0.5 * bias_in[...]
    skip = skip_in[...]

    def mix_token(t, window):
        half = bias + tap[0] * window[0] + tap[1] * window[1] + tap[2] * window[2] + tap[3] * window[3]
        inner = half + half * jnp.tanh(half)
        u_rows[tile(t), :] = dt_rows[tile(t), :] * (inner * LN2)
        y_rows[tile(t), :] = skip * inner

    total = zero
    for t in range(HEAD):
        total = total + dt_rows[tile(t), :]
        sum_rows[tile(t), :] = total
    head_total = total

    def mix(i, carried):
        x0, x1, x2, total = carried
        for k in range(4):
            t = HEAD + i * 4 + k
            x3 = x_rows[tile(t), :]
            mix_token(t, (x0, x1, x2, x3))
            total = total + dt_rows[tile(t), :]
            sum_rows[tile(t), :] = total
            x0, x1, x2 = x1, x2, x3
        return x0, x1, x2, total

    window = tuple(x_rows[tile(t), :] for t in range(HEAD - 3, HEAD))
    *_, total = lax.fori_loop(0, (tokens - HEAD) // 4, mix, window + (total,))

    rate = [rates[tile(n), :] for n in range(states)]

    def advance(t, state):
        step = dt_rows[tile(t), :]
        drive = u_rows[tile(t), :]
        return tuple(jnp.exp2(rate[n] * step) * state[n] + drive * splat(b_splat, n * tokens + t) for n in range(states))

    def local_end(first, steps, state):
        def four(i, state):
            for k in range(4):
                state = advance(first + i * 4 + k, state)
            return state
        return lax.fori_loop(0, steps // 4, four, state)

    half_way = tokens // 2
    state = local_end(HEAD, half_way - HEAD, (zero,) * states)

    pl.semaphore_wait(barrier, LINE - 1 + lines - 1 + jnp.where(me < count - 1, 1, 0))

    @pl.when(me < count - 1)
    def _():
        halo_copy.start()

    state = local_end(half_way, tokens - half_way, state)

    @pl.when(me > 0)
    def _():
        halo_copy.wait_recv()

    @pl.when(me == 0)
    def _():
        halo[...] = jnp.zeros((3 * SUB, LANES), F32)

    window = [halo[tile(t), :] for t in range(3)] + [x_rows[tile(t), :] for t in range(HEAD)]
    for t in range(HEAD):
        mix_token(t, window[t:t + 4])
    early = (zero,) * states
    for t in range(HEAD):
        early = advance(t, early)
    rest = total - head_total
    for n in range(states):
        owner, slot = n // per, n % per
        parts_out[tile(owner * (per + 1) + slot), :] = state[n] + jnp.exp2(rate[n] * rest) * early[n]
    for owner in range(LINE):
        parts_out[tile(owner * (per + 1) + per), :] = total

    size = (per + 1) * SUB
    mine = pl.ds(pl.multiple_of(place * size, SUB), size)
    sent = []
    for step in range(1, LINE):
        target = (place + step) % LINE
        theirs = pl.ds(pl.multiple_of(target * size, SUB), size)
        copy = copy_to(parts_out.at[theirs], parts_in.at[mine], send1.at[step], recv1.at[step], line * LINE + target)
        copy.start()
        sent.append(copy)
    parts_in[mine, :] = parts_out[mine, :]

    def read_out(mine_states):
        def four(i, carried):
            states_now, decays = carried
            for k in range(2):
                t = i * 2 + k
                step = dt_rows[tile(t), :]
                drive = u_rows[tile(t), :]
                y = y_rows[tile(t), :]
                states_next, decays_next = [], []
                for m, n in enumerate(mine_states):
                    decay = jnp.exp2(rates[tile(n), :] * step)
                    read = splat(c_splat, n * tokens + t)
                    now = decay * states_now[m] + drive * splat(b_splat, n * tokens + t)
                    since = decay * decays[m]
                    y = y + read * now
                    decayed[tile(n * tokens + t), :] = read * since
                    states_next.append(now)
                    decays_next.append(since)
                y_rows[tile(t), :] = y
                states_now, decays = tuple(states_next), tuple(decays_next)
            return states_now, decays
        size = len(mine_states)
        lax.fori_loop(0, tokens // 2, four, ((zero,) * size, (one,) * size))

    c_load.wait()
    spread(c_in, c_splat)
    read_out(SHARES[0])

    for copy in sent:
        copy.wait_recv()
    own_rate = [rates[tile(place * per + m), :] for m in range(per)]
    ahead = [zero] * per
    span = zero
    for other in range(LINE):
        step = parts_in[tile(other * (per + 1) + per), :]
        for m in range(per):
            starts_out[tile(other * per + m), :] = ahead[m]
            spans[tile(other * per + m), :] = jnp.exp2(own_rate[m] * span)
            ahead[m] = jnp.exp2(own_rate[m] * step) * ahead[m] + parts_in[tile(other * (per + 1) + m), :]
        span = span + step
    for m in range(per):
        total_out[tile(m), :] = ahead[m]
    total_out[tile(per), :] = span

    my_line = pl.ds(pl.multiple_of(line * size, SUB), size)

    def line_copy(step):
        return copy_to(total_out, total_in.at[my_line], send2.at[step], recv2.at[step], (line + step) * LINE + place)

    for step in range(1, lines):
        @pl.when(line + step < lines)
        def _():
            line_copy(step).start()

    z_load.wait()

    def gates(i, _):
        rows = pl.ds(pl.multiple_of(i * 16, 16), 16)
        for j in range(groups):
            half = 0.5 * z_in[rows, j * LANES:(j + 1) * LANES].astype(F32)
            gate[rows, j * LANES:(j + 1) * LANES] = half + half * jnp.tanh(half)
        return 0

    lax.fori_loop(0, tokens // 16, gates, 0)
    read_out(SHARES[1])

    for m in range(per):
        carry[tile(m), :] = zero
    for step in range(lines - 1, 0, -1):
        @pl.when(line >= step)
        def _():
            line_copy(step).wait_recv()
            first = (line - step) * (per + 1)
            step_sum = total_in[tile(first + per), :]
            for m in range(per):
                decay = jnp.exp2(own_rate[m] * step_sum)
                carry[tile(m), :] = decay * carry[tile(m), :] + total_in[tile(first + m), :]

    for other in range(LINE):
        for m in range(per):
            at = tile(other * per + m)
            starts_out[at, :] = starts_out[at, :] + spans[at, :] * carry[tile(m), :]
    returned = []
    mine = tile(place * per, per)
    for step in range(1, LINE):
        target = (place + step) % LINE
        copy = copy_to(starts_out.at[tile(target * per, per)], starts.at[mine], send3.at[step], recv3.at[step],
                       line * LINE + target)
        copy.start()
        returned.append(copy)
    starts[mine, :] = starts_out[mine, :]

    read_out(SHARES[2])

    for copy in returned:
        copy.wait_recv()
    start = [starts[tile(n), :] for n in range(states)]

    def finish(i, _):
        for k in range(16):
            t = i * 16 + k
            terms = [decayed[tile(n * tokens + t), :] * start[n] for n in range(states)] + [y_rows[tile(t), :]]
            while len(terms) > 1:
                terms = [terms[q] + terms[q + 1] if q + 1 < len(terms) else terms[q] for q in range(0, len(terms), 2)]
            y_rows[tile(t), :] = terms[0]
        rows = pl.ds(pl.multiple_of(i * 16, 16), 16)
        for j in range(groups):
            mixed = y_rows[pl.ds(i * 16 * SUB + j, 16, stride=SUB), :]
            at = slice(j * LANES, (j + 1) * LANES)
            out_ref[rows, at] = (mixed * gate[rows, at]).astype(jnp.bfloat16)
        return 0

    lax.fori_loop(0, tokens // 16, finish, 0)

    @pl.when(me < count - 1)
    def _():
        halo_copy.wait_send()

    for copy in sent + returned:
        copy.wait_send()
    for step in range(1, lines):
        @pl.when(line + step < lines)
        def _():
            line_copy(step).wait_send()


def solution(mesh):
    count = mesh.shape["ctx"]
    lines = count // LINE

    def body(x_in, z_gate, dt_raw, b_proj, c_proj, conv_weight, conv_bias, a_log, d_skip):
        tokens, channels = x_in.shape
        states = a_log.shape[0]
        per = states // LINE
        groups = channels // LANES

        def block(*shape, dtype=F32):
            return pltpu.VMEM(shape, dtype)

        def rows(number):
            return block(number * SUB, LANES)

        bf16 = functools.partial(block, dtype=jnp.bfloat16)
        scratch = [
            bf16(tokens, channels), bf16(tokens, channels), bf16(tokens, channels), bf16(states, tokens), bf16(states, tokens),
            block(4, channels), block(SUB, LANES), block(states, channels), block(SUB, LANES),
            rows(tokens), rows(tokens), rows(tokens), rows(tokens), rows(tokens), block(tokens, channels),
            block(states * tokens + SUB, LANES), block(states * tokens + SUB, LANES), rows(states), rows(4),
            rows(states * tokens), rows(states),
            rows(3), rows(LINE * (per + 1)), rows(LINE * (per + 1)), rows(per + 1), rows(lines * (per + 1)), rows(per),
            rows(states), rows(states), rows(states),
            pltpu.SemaphoreType.DMA((9,)), pltpu.SemaphoreType.DMA((2,)),
            pltpu.SemaphoreType.DMA((LINE,)), pltpu.SemaphoreType.DMA((LINE,)),
            pltpu.SemaphoreType.DMA((lines,)), pltpu.SemaphoreType.DMA((lines,)),
            pltpu.SemaphoreType.DMA((LINE,)), pltpu.SemaphoreType.DMA((LINE,)),
        ]
        return pl.pallas_call(
            functools.partial(kernel, lines),
            out_shape=jax.ShapeDtypeStruct((tokens, channels), jnp.bfloat16),
            in_specs=[pl.BlockSpec(memory_space=pltpu.HBM)] * 9,
            out_specs=pl.BlockSpec(memory_space=pltpu.VMEM),
            scratch_shapes=scratch,
            compiler_params=pltpu.CompilerParams(
                collective_id=0, has_side_effects=True, vmem_limit_bytes=48 * 2**20
            ),
        )(x_in, z_gate, dt_raw, b_proj.T, c_proj.T, conv_weight, conv_bias.reshape(groups, LANES), a_log,
          d_skip.reshape(groups, LANES))

    in_specs = (
        P("ctx", "mp"),
        P("ctx", "mp"),
        P("ctx", "mp"),
        P("ctx", None),
        P("ctx", None),
        P(None, "mp"),
        P("mp"),
        P(None, "mp"),
        P("mp"),
    )
    return jax.shard_map(body, mesh=mesh, in_specs=in_specs, out_specs=P("ctx", "mp"), check_vma=False)
```

time: 995 us -> 37.1 us (0.04)
  the two profiles are of different devices: /device:TPU:126 before, /device:TPU:448 now
where the time goes in v1:
time: 37.1 us; the launch traced here: 36.6 us
  Pallas kernels  28.3 us (76%)
  local copies, waits for them, and re-layouts  8.24 us (22%)
    pallas_call x1, Pallas kernels, body(): pl.pallas_call(functools.partial(kernel, lines), out_shape=jax.ShapeDtype...  28.3 us
    unnamed x19, local copies, waits for them, and re-layouts  8.24 us

profile of v1, /device:TPU:448, one launch (start us, length us, event | category | flops | bytes accessed | tf_op | source)
XLA Modules:
  0.0 36.6 jit_solution(6238751072685922671)
XLA Ops:
  0.0 0.0 copy-start.7
  0.0 0.7 %copy-done.7 = f32[1024]{0:T(1024)S(1)} copy-done((f32[1024]{0:T(1024)S(1)}, f32[1024]{0:T(1024)}, u32[]{:S(2)}) %copy-start.7) | copy-done | bytes 4120
  0.7 0.0 copy-start
  0.7 1.0 %copy-done = bf16[256,1024]{1,0:T(8,128)(2,1)S(1)} copy-done((bf16[256,1024]{1,0:T(8,128)(2,1)S(1)}, bf16[256,1024]{1,0:T(8,128)(2,1)}, u32[]{:S(2)}) %copy-start) | copy-done | bytes 524312
  1.7 0.0 copy-start.1
  1.7 1.0 %copy-done.1 = bf16[256,1024]{1,0:T(8,128)(2,1)S(1)} copy-done((bf16[256,1024]{1,0:T(8,128)(2,1)S(1)}, bf16[256,1024]{1,0:T(8,128)(2,1)}, u32[]{:S(2)}) %copy-start.1) | copy-done | bytes 524312
  2.8 0.0 copy-start.2
  2.8 1.0 %copy-done.2 = bf16[256,1024]{1,0:T(8,128)(2,1)S(1)} copy-done((bf16[256,1024]{1,0:T(8,128)(2,1)S(1)}, bf16[256,1024]{1,0:T(8,128)(2,1)}, u32[]{:S(2)}) %copy-start.2) | copy-done | bytes 524312
  3.8 0.0 copy-start.3
  3.8 0.8 %copy-done.3 = f32[16,1024]{1,0:T(8,128)S(1)} copy-done((f32[16,1024]{1,0:T(8,128)S(1)}, f32[16,1024]{1,0:T(8,128)}, u32[]{:S(2)}) %copy-start.3) | copy-done | bytes 65560
  4.7 0.0 copy-start.4
  4.7 0.7 %copy-done.4 = f32[4,1024]{1,0:T(4,128)S(1)} copy-done((f32[4,1024]{1,0:T(4,128)S(1)}, f32[4,1024]{1,0:T(4,128)}, u32[]{:S(2)}) %copy-start.4) | copy-done | bytes 16408
  5.4 0.0 copy-start.5
  5.4 0.7 %copy-done.5 = bf16[256,16]{0,1:T(8,128)(2,1)S(1)} copy-done((bf16[256,16]{0,1:T(8,128)(2,1)S(1)}, bf16[256,16]{0,1:T(8,128)(2,1)}, u32[]{:S(2)}) %copy-start.5) | copy-done | bytes 8216
  6.1 0.0 copy-start.6
  6.1 0.7 %copy-done.6 = bf16[256,16]{0,1:T(8,128)(2,1)S(1)} copy-done((bf16[256,16]{0,1:T(8,128)(2,1)S(1)}, bf16[256,16]{0,1:T(8,128)(2,1)}, u32[]{:S(2)}) %copy-start.6) | copy-done | bytes 8216
  6.8 0.0 copy-start.8
  6.8 0.7 %copy-done.8 = f32[1024]{0:T(1024)S(1)} copy-done((f32[1024]{0:T(1024)S(1)}, f32[1024]{0:T(1024)}, u32[]{:S(2)}) %copy-start.8) | copy-done | bytes 4120
  7.5 28.3 %shard_map.91 = bf16[256,1024]{1,0:T(8,128)(2,1)S(1)} custom-call(bf16[256,1024]{1,0:T(8,128)(2,1)S(1)} %copy-done, bf16[256,1024]{1,0:T(8,128)(2,1)S(1)} %copy-done.1, bf16[256,1024]{1,0:T(8,128)(2,1)S(1)} %copy-done.2, bf16[16,256]{1,0:T(8,128)(2,1)S(1)} %bitcast.4, bf16[16,256]{1,0:T(8,128)(2,1)S(1)} %bitcast.5, f32[4,1024]{1,0:T(4,128)S(1)} %copy-done.4, ...), custom_call_target="tpu_custom_call" | custom-call | tf_op jit(solution)/shard_map/pallas_call | solution.py:360
  35.8 0.8 %copy.11 = bf16[256,1024]{1,0:T(8,128)(2,1)} copy(bf16[256,1024]{1,0:T(8,128)(2,1)S(1)} %shard_map.91) | data formatting | bytes 1048576
Async XLA Ops:
  0.0 0.7 %copy-start.7 = (f32[1024]{0:T(1024)S(1)}, f32[1024]{0:T(1024)}, u32[]{:S(2)}) copy-start(f32[1024]{0:T(1024)} %param.15) | copy-start | bytes 12292
  0.7 1.0 %copy-start = (bf16[256,1024]{1,0:T(8,128)(2,1)S(1)}, bf16[256,1024]{1,0:T(8,128)(2,1)}, u32[]{:S(2)}) copy-start(bf16[256,1024]{1,0:T(8,128)(2,1)} %x_hbm.1) | copy-start | bytes 1572868
  1.7 1.0 %copy-start.1 = (bf16[256,1024]{1,0:T(8,128)(2,1)S(1)}, bf16[256,1024]{1,0:T(8,128)(2,1)}, u32[]{:S(2)}) copy-start(bf16[256,1024]{1,0:T(8,128)(2,1)} %z_hbm.1) | copy-start | bytes 1572868
  2.8 1.0 %copy-start.2 = (bf16[256,1024]{1,0:T(8,128)(2,1)S(1)}, bf16[256,1024]{1,0:T(8,128)(2,1)}, u32[]{:S(2)}) copy-start(bf16[256,1024]{1,0:T(8,128)(2,1)} %dt_hbm.1) | copy-start | bytes 1572868
  3.8 0.8 %copy-start.3 = (f32[16,1024]{1,0:T(8,128)S(1)}, f32[16,1024]{1,0:T(8,128)}, u32[]{:S(2)}) copy-start(f32[16,1024]{1,0:T(8,128)} %a_hbm.1) | copy-start | bytes 196612
  4.7 0.7 %copy-start.4 = (f32[4,1024]{1,0:T(4,128)S(1)}, f32[4,1024]{1,0:T(4,128)}, u32[]{:S(2)}) copy-start(f32[4,1024]{1,0:T(4,128)} %w_hbm.1) | copy-start | bytes 49156
  5.4 0.7 %copy-start.5 = (bf16[256,16]{0,1:T(8,128)(2,1)S(1)}, bf16[256,16]{0,1:T(8,128)(2,1)}, u32[]{:S(2)}) copy-start(bf16[256,16]{0,1:T(8,128)(2,1)} %param.12) | copy-start | bytes 24580
  6.1 0.7 %copy-start.6 = (bf16[256,16]{0,1:T(8,128)(2,1)S(1)}, bf16[256,16]{0,1:T(8,128)(2,1)}, u32[]{:S(2)}) copy-start(bf16[256,16]{0,1:T(8,128)(2,1)} %param.13) | copy-start | bytes 24580
  6.8 0.7 %copy-start.8 = (f32[1024]{0:T(1024)S(1)}, f32[1024]{0:T(1024)}, u32[]{:S(2)}) copy-start(f32[1024]{0:T(1024)} %param.17) | copy-start | bytes 12292

commit v2 on v1

v2 whole, which is shorter than its diff:
```python
import functools

import jax
import jax.numpy as jnp
from jax import lax
from jax.experimental import pallas as pl
from jax.experimental.pallas import tpu as pltpu
from jax.sharding import PartitionSpec as P

MESH = pl.DeviceIdType.MESH
F32 = jnp.float32
LANES = 128
SUB = 8
LINE = 8
HEAD = 4
LINE_RANKS = (0, 1, 4, 5, 2, 3, 6, 7)
MIX = 12
SCAN = 28
LOG2E = 1.4426950408889634
LN2 = 0.6931471805599453
SHARES = ((0, 1, 2, 3, 4, 5, 6, 7), (8, 9, 10, 11), (12, 13, 14, 15))


def tile(index, count=1):
    if isinstance(index, int):
        return pl.ds(index * SUB, count * SUB)
    return pl.ds(pl.multiple_of(index * SUB, SUB), count * SUB)


def splat(ref, index):
    return ref[pl.ds(index, SUB, stride=0), :]


def kernel(lines, x_hbm, z_hbm, dt_hbm, b_hbm, c_hbm, w_hbm, bias_hbm, a_hbm, skip_hbm, out_ref,
           x_in, z_in, dt_in, b_in, c_in, w_in, bias_in, a_in, skip_in,
           x_rows, dt_rows, u_rows, y_rows, gate, b_splat, c_splat, rates, taps, decayed,
           halo, parts_out, parts_in, total_out, total_in, carry, spans, starts_out, starts,
           load_sem, place_sem, line_sem, halo_sem, send1, recv1, send2, recv2, send3, recv3):
    tokens, channels = x_in.shape
    states = a_in.shape[0]
    per = states // LINE
    groups = channels // LANES
    me = lax.axis_index("ctx")
    line, place = me // LINE, me % LINE
    count = lines * LINE

    pairs = ((b_hbm, b_in), (a_hbm, a_in), (dt_hbm, dt_in), (x_hbm, x_in), (w_hbm, w_in),
             (bias_hbm, bias_in), (skip_hbm, skip_in), (c_hbm, c_in), (z_hbm, z_in))
    loads = [pltpu.make_async_copy(src, dst, load_sem.at[i]) for i, (src, dst) in enumerate(pairs)]
    for load in loads:
        load.start()
    b_load, a_load, dt_load, x_load, w_load, bias_load, skip_load, c_load, z_load = loads

    mp = lax.axis_index("mp")
    late_line, late_column = (mp == 0) & (line == 0), (mp == 0) & (place == 0)

    def place_rank(at):
        rank = jnp.where(at < LINE // 2, at, LINE + LINE // 2 - 1 - at)
        return jnp.where(late_line, jnp.where(at == 0, LINE - 1, rank - 1), rank)

    def line_rank(at):
        rank = 0
        for other, value in enumerate(LINE_RANKS):
            rank = rank + jnp.where(at == other, value, 0)
        return jnp.where(late_column, jnp.where(at == 0, lines - 1, rank - 1), rank)

    my_place_rank, my_line_rank = place_rank(place), line_rank(line)
    barrier = pltpu.get_barrier_semaphore()

    def signal(semaphore, target):
        pl.semaphore_signal(semaphore, inc=1, device_id={"ctx": target}, device_id_type=MESH)

    for step in range(1, LINE):
        target = (place + step) % LINE

        @pl.when(place_rank(target) > my_place_rank)
        def _():
            signal(barrier, line * LINE + target)
    for other in range(lines):
        @pl.when(line_rank(other) > my_line_rank)
        def _():
            signal(barrier, other * LINE + place)

    @pl.when(jnp.where(place == 0, line > 0, place_rank(place - 1) < my_place_rank))
    def _():
        signal(barrier, me - 1)

    def greet():
        after = jnp.where(place == LINE - 1, me < count - 1, place_rank(place + 1) > my_place_rank)
        pl.semaphore_wait(barrier, my_place_rank + my_line_rank + jnp.where(after, 1, 0))
        for step in range(1, LINE):
            target = (place + step) % LINE

            greeted = (place > 0) if step == LINE - 1 else False

            @pl.when((place_rank(target) < my_place_rank) & jnp.logical_not(greeted))
            def _():
                signal(place_sem.at[LINE - step], line * LINE + target)
        for step in range(1, lines):
            @pl.when((line >= step) & (line_rank(line - step) < my_line_rank))
            def _():
                signal(line_sem.at[step], (line - step) * LINE + place)

    def know_place(step):
        known = (place < LINE - 1) if step == 1 else False

        @pl.when((place_rank((place + step) % LINE) > my_place_rank) & jnp.logical_not(known))
        def _():
            pl.semaphore_wait(place_sem.at[step], 1)

    def know_line(step):
        @pl.when(line_rank(line + step) > my_line_rank)
        def _():
            pl.semaphore_wait(line_sem.at[step], 1)

    def copy_to(src, dst, send, recv, target):
        return pltpu.make_async_remote_copy(src_ref=src, dst_ref=dst, send_sem=send, recv_sem=recv,
                                            device_id={"ctx": target}, device_id_type=MESH)

    halo_copy = copy_to(x_rows.at[pl.ds((tokens - 3) * SUB, 3 * SUB)], halo, halo_sem.at[0], halo_sem.at[1], me + 1)

    zero = jnp.zeros((SUB, LANES), F32)
    one = jnp.ones((SUB, LANES), F32)

    def spread(src, dst, scale=None):
        wide = 2 * LANES
        for n in range(0, states, 2):
            state_of = lax.broadcasted_iota(jnp.int32, (states, wide), 0)
            lane = lax.broadcasted_iota(jnp.int32, (states, wide), 1)
            pick = jnp.where(state_of == n + lane // LANES, 1.0, 0.0).astype(jnp.bfloat16)
            both = lax.dot_general(src[...], pick, (((0,), (0,)), ((), ())), preferred_element_type=F32)
            if scale is not None:
                both = both * scale
            dst[n * tokens:(n + 1) * tokens, :] = both[:, :LANES]
            dst[(n + 1) * tokens:(n + 2) * tokens, :] = both[:, LANES:]

    b_load.wait()
    spread(b_in, b_splat)

    a_load.wait()
    for j in range(groups):
        rates[pl.ds(j, states, stride=SUB), :] = -jnp.exp(a_in[:, j * LANES:(j + 1) * LANES])

    soon = ((place >= LINE // 2) & (place < LINE - 1)) | (late_line & (place == 0))
    pl.when(soon)(greet)
    dt_load.wait()

    def step_sizes(i, _):
        rows = pl.ds(pl.multiple_of(i * 32, 32), 32)
        for j in range(groups):
            raw = dt_in[rows, j * LANES:(j + 1) * LANES].astype(F32)
            dt_rows[pl.ds(i * 32 * SUB + j, 32, stride=SUB), :] = jnp.log2(1.0 + jnp.exp2(raw * LOG2E))
        return 0

    lax.fori_loop(0, tokens // 32, step_sizes, 0)

    x_load.wait()

    def lay_out(i, _):
        rows = pl.ds(pl.multiple_of(i * 32, 32), 32)
        for j in range(groups):
            x_rows[pl.ds(i * 32 * SUB + j, 32, stride=SUB), :] = x_in[rows, j * LANES:(j + 1) * LANES].astype(F32)
        return 0

    lax.fori_loop(0, tokens // 32, lay_out, 0)
    pl.when(jnp.logical_not(soon))(greet)

    @pl.when(me < count - 1)
    def _():
        halo_copy.start()

    w_load.wait()
    bias_load.wait()
    skip_load.wait()
    for j in range(groups):
        taps[pl.ds(j, 4, stride=SUB), :] = 0.5 * w_in[:, j * LANES:(j + 1) * LANES]
    tap = [taps[tile(k), :] for k in range(4)]
    bias = 0.5 * bias_in[...]

    def mix_token(t, window):
        half = bias + tap[0] * window[0] + tap[1] * window[1] + tap[2] * window[2] + tap[3] * window[3]
        inner = half + half * jnp.tanh(half)
        u_rows[tile(t), :] = dt_rows[tile(t), :] * inner
        y_rows[tile(t), :] = inner

    total = zero
    for t in range(HEAD):
        total = total + dt_rows[tile(t), :]
    head_total = total

    def mix(i, carried):
        x0, x1, x2, total = carried
        for k in range(MIX):
            t = HEAD + i * MIX + k
            x3 = x_rows[tile(t), :]
            mix_token(t, (x0, x1, x2, x3))
            total = total + dt_rows[tile(t), :]
            x0, x1, x2 = x1, x2, x3
        return x0, x1, x2, total

    window = tuple(x_rows[tile(t), :] for t in range(HEAD - 3, HEAD))
    *_, total = lax.fori_loop(0, (tokens - HEAD) // MIX, mix, window + (total,))

    def advance(group, t, state):
        step = dt_rows[tile(t), :]
        drive = u_rows[tile(t), :]
        return tuple(jnp.exp2(rates[tile(n), :] * step) * now + drive * splat(b_splat, n * tokens + t)
                     for n, now in zip(group, state))

    def local_end(group):
        def some(i, state):
            for k in range(SCAN):
                state = advance(group, HEAD + i * SCAN + k, state)
            return state
        return lax.fori_loop(0, (tokens - HEAD) // SCAN, some, (zero,) * len(group))

    halves = (range(states // 2), range(states // 2, states))
    state = local_end(halves[0])

    state = state + local_end(halves[1])

    @pl.when(me > 0)
    def _():
        halo_copy.wait_recv()

    @pl.when(me == 0)
    def _():
        halo[...] = jnp.zeros((3 * SUB, LANES), F32)

    window = [halo[tile(t), :] for t in range(3)] + [x_rows[tile(t), :] for t in range(HEAD)]
    for t in range(HEAD):
        mix_token(t, window[t:t + 4])
    early = (zero,) * states
    for t in range(HEAD):
        early = advance(range(states), t, early)
    rest = total - head_total
    for n in range(states):
        owner, slot = n // per, n % per
        parts_out[tile(owner * (per + 1) + slot), :] = state[n] + jnp.exp2(rates[tile(n), :] * rest) * early[n]
    for owner in range(LINE):
        parts_out[tile(owner * (per + 1) + per), :] = total

    size = (per + 1) * SUB
    mine = pl.ds(pl.multiple_of(place * size, SUB), size)
    sent = []
    for step in (1, LINE - 1, 2, LINE - 2, 3, LINE - 3, LINE // 2):
        know_place(step)
        target = (place + step) % LINE
        theirs = pl.ds(pl.multiple_of(target * size, SUB), size)
        copy = copy_to(parts_out.at[theirs], parts_in.at[mine], send1.at[step], recv1.at[step], line * LINE + target)
        copy.start()
        sent.append(copy)
    parts_in[mine, :] = parts_out[mine, :]

    skip = skip_in[...]

    def read_out(mine_states):
        steps = 64 // len(mine_states)

        def some(i, carried):
            states_now, decays = carried
            for k in range(steps):
                t = i * steps + k
                step = dt_rows[tile(t), :]
                drive = u_rows[tile(t), :]
                y = y_rows[tile(t), :]
                if 0 in mine_states:
                    y = skip * y
                states_next, decays_next = [], []
                for m, n in enumerate(mine_states):
                    decay = jnp.exp2(rates[tile(n), :] * step)
                    read = splat(c_splat, n * tokens + t)
                    now = decay * states_now[m] + drive * splat(b_splat, n * tokens + t)
                    since = decay * decays[m]
                    y = y + read * now
                    decayed[tile(t * states + n), :] = read * since
                    states_next.append(now)
                    decays_next.append(since)
                y_rows[tile(t), :] = y
                states_now, decays = tuple(states_next), tuple(decays_next)
            return states_now, decays
        size = len(mine_states)
        lax.fori_loop(0, tokens // steps, some, ((zero,) * size, (one,) * size))

    c_load.wait()
    spread(c_in, c_splat, LN2)
    read_out(SHARES[0])
    z_load.wait()

    def gates(i, _):
        rows = pl.ds(pl.multiple_of(i * 16, 16), 16)
        for j in range(groups):
            half = 0.5 * z_in[rows, j * LANES:(j + 1) * LANES].astype(F32)
            gate[rows, j * LANES:(j + 1) * LANES] = half + half * jnp.tanh(half)
        return 0

    lax.fori_loop(0, tokens // 16, gates, 0)

    for copy in sent:
        copy.wait_recv()
    own_rate = [rates[tile(place * per + m), :] for m in range(per)]
    ahead = [zero] * per
    span = zero
    for other in range(LINE):
        step = parts_in[tile(other * (per + 1) + per), :]
        for m in range(per):
            starts_out[tile(other * per + m), :] = ahead[m]
            spans[tile(other * per + m), :] = jnp.exp2(own_rate[m] * span)
            ahead[m] = jnp.exp2(own_rate[m] * step) * ahead[m] + parts_in[tile(other * (per + 1) + m), :]
        span = span + step
    for m in range(per):
        total_out[tile(m), :] = ahead[m]
    total_out[tile(per), :] = span

    my_line = pl.ds(pl.multiple_of(line * size, SUB), size)

    def line_copy(step):
        return copy_to(total_out, total_in.at[my_line], send2.at[step], recv2.at[step], (line + step) * LINE + place)

    for step in range(1, lines):
        @pl.when(line + step < lines)
        def _():
            know_line(step)
            line_copy(step).start()


    for m in range(per):
        carry[tile(m), :] = zero
    for step in range(lines - 1, 0, -1):
        @pl.when(line >= step)
        def _():
            line_copy(step).wait_recv()
            first = (line - step) * (per + 1)
            step_sum = total_in[tile(first + per), :]
            for m in range(per):
                decay = jnp.exp2(own_rate[m] * step_sum)
                carry[tile(m), :] = decay * carry[tile(m), :] + total_in[tile(first + m), :]

    for other in range(LINE):
        for m in range(per):
            at = tile(other * per + m)
            starts_out[at, :] = starts_out[at, :] + spans[at, :] * carry[tile(m), :]
    returned = []
    mine = tile(place * per, per)
    for step in range(1, LINE):
        target = (place + step) % LINE
        copy = copy_to(starts_out.at[tile(target * per, per)], starts.at[mine], send3.at[step], recv3.at[step],
                       line * LINE + target)
        copy.start()
        returned.append(copy)
    starts[mine, :] = starts_out[mine, :]

    read_out(SHARES[1])
    read_out(SHARES[2])

    def start_terms(owners, t):
        terms = []
        for first, start in owners:
            for m in range(per):
                terms.append(decayed[tile(t * states + first + m), :] * start[m])
        return terms

    def tree(terms):
        while len(terms) > 1:
            terms = [terms[q] + terms[q + 1] if q + 1 < len(terms) else terms[q] for q in range(0, len(terms), 2)]
        return terms[0]

    def arrived(steps):
        owners = []
        for step in steps:
            if step:
                returned[step - 1].wait_recv()
            first = ((place + LINE - step) % LINE) * per
            owners.append((first, [starts[tile(first + m), :] for m in range(per)]))
        return owners

    for steps in ((0, 1, LINE - 1), (2, LINE - 2), (3, LINE - 3)):
        owners = arrived(steps)

        def add(i, _):
            for k in range(16):
                t = i * 16 + k
                y_rows[tile(t), :] = tree(start_terms(owners, t) + [y_rows[tile(t), :]])
            return 0

        lax.fori_loop(0, tokens // 16, add, 0)
    far = arrived((LINE // 2,))

    def finish(i, _):
        for k in range(16):
            t = i * 16 + k
            y_rows[tile(t), :] = tree(start_terms(far, t) + [y_rows[tile(t), :]])
        rows = pl.ds(pl.multiple_of(i * 16, 16), 16)
        for j in range(groups):
            mixed = y_rows[pl.ds(i * 16 * SUB + j, 16, stride=SUB), :]
            at = slice(j * LANES, (j + 1) * LANES)
            out_ref[rows, at] = (mixed * gate[rows, at]).astype(jnp.bfloat16)
        return 0

    lax.fori_loop(0, tokens // 16, finish, 0)

    @pl.when(me < count - 1)
    def _():
        halo_copy.wait_send()

    for copy in sent + returned:
        copy.wait_send()
    for step in range(1, lines):
        @pl.when(line + step < lines)
        def _():
            line_copy(step).wait_send()


def solution(mesh):
    count = mesh.shape["ctx"]
    lines = count // LINE

    def body(x_in, z_gate, dt_raw, b_proj, c_proj, conv_weight, conv_bias, a_log, d_skip):
        tokens, channels = x_in.shape
        states = a_log.shape[0]
        per = states // LINE
        groups = channels // LANES

        def block(*shape, dtype=F32):
            return pltpu.VMEM(shape, dtype)

        def rows(number):
            return block(number * SUB, LANES)

        bf16 = functools.partial(block, dtype=jnp.bfloat16)
        scratch = [
            bf16(tokens, channels), bf16(tokens, channels), bf16(tokens, channels), bf16(states, tokens), bf16(states, tokens),
            block(4, channels), block(SUB, LANES), block(states, channels), block(SUB, LANES),
            rows(tokens), rows(tokens), rows(tokens), rows(tokens), block(tokens, channels),
            block(states * tokens + SUB, LANES), block(states * tokens + SUB, LANES), rows(states), rows(4),
            rows(states * tokens),
            rows(3), rows(LINE * (per + 1)), rows(LINE * (per + 1)), rows(per + 1), rows(lines * (per + 1)), rows(per),
            rows(states), rows(states), rows(states),
            pltpu.SemaphoreType.DMA((9,)), pltpu.SemaphoreType.REGULAR((LINE,)),
            pltpu.SemaphoreType.REGULAR((lines,)), pltpu.SemaphoreType.DMA((2,)),
            pltpu.SemaphoreType.DMA((LINE,)), pltpu.SemaphoreType.DMA((LINE,)),
            pltpu.SemaphoreType.DMA((lines,)), pltpu.SemaphoreType.DMA((lines,)),
            pltpu.SemaphoreType.DMA((LINE,)), pltpu.SemaphoreType.DMA((LINE,)),
        ]
        operands = (x_in, z_gate, dt_raw, b_proj.T, c_proj.T, conv_weight, conv_bias.reshape(groups, LANES), a_log,
                    d_skip.reshape(groups, LANES))
        return pl.pallas_call(
            functools.partial(kernel, lines),
            out_shape=pltpu.VMEM((tokens, channels), jnp.bfloat16),
            in_specs=[pl.BlockSpec(memory_space=pltpu.HBM)] * 9,
            out_specs=pl.BlockSpec(memory_space=pltpu.VMEM),
            scratch_shapes=scratch,
            compiler_params=pltpu.CompilerParams(
                collective_id=0, has_side_effects=True, vmem_limit_bytes=48 * 2**20
            ),
        )(*(pltpu.with_memory_space_constraint(operand, pltpu.HBM) for operand in operands))

    in_specs = (
        P("ctx", "mp"),
        P("ctx", "mp"),
        P("ctx", "mp"),
        P("ctx", None),
        P("ctx", None),
        P(None, "mp"),
        P("mp"),
        P(None, "mp"),
        P("mp"),
    )
    return jax.shard_map(body, mesh=mesh, in_specs=in_specs, out_specs=P("ctx", "mp"), check_vma=False)
```

time: 37.1 us -> 26.8 us (0.72)
  local copies, waits for them, and re-layouts: 8.24 us -> 0.8 us
  Pallas kernels: 28.3 us -> 25.8 us
    unnamed x19 -> x1, local copies, waits for them, and re-layouts: 8.24 us -> 0.8 us
    pallas_call x1, Pallas kernels: 28.3 us -> 25.8 us  [body(): pl.pallas_call(functools.partial(kernel, lines), out_shape=pltpu.VMEM((to...]
where the time goes in v2:
time: 26.8 us; the launch traced here: 26.6 us
  Pallas kernels  25.8 us (96%)
  local copies, waits for them, and re-layouts  0.8 us (3%)
    pallas_call x1, Pallas kernels, body(): pl.pallas_call(functools.partial(kernel, lines), out_shape=pltpu.VMEM((to...  25.8 us
    unnamed x1, local copies, waits for them, and re-layouts  0.8 us

profile of v2, /device:TPU:448, one launch (start us, length us, event | category | flops | bytes accessed | tf_op | source)
XLA Modules:
  0.0 26.6 jit_solution(10636992181642981420)
XLA Ops:
  0.0 25.8 %shard_map.91 = bf16[256,1024]{1,0:T(8,128)(2,1)S(1)} custom-call(bf16[256,1024]{1,0:T(8,128)(2,1)} %x_hbm.1, bf16[256,1024]{1,0:T(8,128)(2,1)} %z_hbm.1, bf16[256,1024]{1,0:T(8,128)(2,1)} %dt_hbm.1, bf16[16,256]{1,0:T(8,128)(2,1)} %bitcast.4, bf16[16,256]{1,0:T(8,128)(2,1)} %bitcast.5, f32[4,1024]{1,0:T(4,128)} %w_hbm.1, f32[8,128]{1,0:T(8,128)} %bitcast.6, ...), custom_call_target="tpu_custom_call" | custom-call | tf_op jit(solution)/shard_map/pallas_call | solution.py:447
  25.8 0.8 %copy.11 = bf16[256,1024]{1,0:T(8,128)(2,1)} copy(bf16[256,1024]{1,0:T(8,128)(2,1)S(1)} %shard_map.91) | data formatting | bytes 1048576

commit v3 on v2

--- a/solution.py
+++ b/solution.py
@@ -14,11 +14,12 @@
 LINE = 8
 HEAD = 4
 LINE_RANKS = (0, 1, 4, 5, 2, 3, 6, 7)
-MIX = 12
-SCAN = 28
+FAR_FIRST = (4, 3, 5, 2, 6, 1, 7)
+BLOCK = 32
+SCAN = 42
 LOG2E = 1.4426950408889634
 LN2 = 0.6931471805599453
-SHARES = ((0, 1, 2, 3, 4, 5, 6, 7), (8, 9, 10, 11), (12, 13, 14, 15))
+SHARES = ((0, 1, 2, 3), (4, 5, 6, 7), (8, 9, 10, 11, 12, 13, 14, 15))
 
 
 def tile(index, count=1):
@@ -35,7 +36,7 @@
            x_in, z_in, dt_in, b_in, c_in, w_in, bias_in, a_in, skip_in,
            x_rows, dt_rows, u_rows, y_rows, gate, b_splat, c_splat, rates, taps, decayed,
            halo, parts_out, parts_in, total_out, total_in, carry, spans, starts_out, starts,
-           load_sem, place_sem, line_sem, halo_sem, send1, recv1, send2, recv2, send3, recv3):
+           load_sem, dt_sem, x_sem, place_sem, line_sem, halo_sem, send1, recv1, send2, recv2, send3, recv3):
     tokens, channels = x_in.shape
     states = a_in.shape[0]
     per = states // LINE
@@ -44,12 +45,26 @@
     line, place = me // LINE, me % LINE
     count = lines * LINE
 
-    pairs = ((b_hbm, b_in), (a_hbm, a_in), (dt_hbm, dt_in), (x_hbm, x_in), (w_hbm, w_in),
+    pairs = ((b_hbm, b_in), (a_hbm, a_in), (w_hbm, w_in),
              (bias_hbm, bias_in), (skip_hbm, skip_in), (c_hbm, c_in), (z_hbm, z_in))
     loads = [pltpu.make_async_copy(src, dst, load_sem.at[i]) for i, (src, dst) in enumerate(pairs)]
-    for load in loads:
+    blocks = tokens // BLOCK
+
+    def chunk(i, src, dst, sem):
+        rows = pl.ds(pl.multiple_of(i * BLOCK, BLOCK), BLOCK)
+        return pltpu.make_async_copy(src.at[rows], dst.at[rows], sem.at[i])
+
+    def chunks(i):
+        return chunk(i, dt_hbm, dt_in, dt_sem), chunk(i, x_hbm, x_in, x_sem)
+
+    for load in loads[:2]:
         load.start()
-    b_load, a_load, dt_load, x_load, w_load, bias_load, skip_load, c_load, z_load = loads
+    for i in range(blocks):
+        for load in chunks(i):
+            load.start()
+    for load in loads[2:]:
+        load.start()
+    b_load, a_load, w_load, bias_load, skip_load, c_load, z_load = loads
 
     mp = lax.axis_index("mp")
     late_line, late_column = (mp == 0) & (line == 0), (mp == 0) & (place == 0)
@@ -143,32 +158,17 @@
 
     soon = ((place >= LINE // 2) & (place < LINE - 1)) | (late_line & (place == 0))
     pl.when(soon)(greet)
-    dt_load.wait()
-
-    def step_sizes(i, _):
-        rows = pl.ds(pl.multiple_of(i * 32, 32), 32)
+    def lay_out(i):
+        for load in chunks(i):
+            load.wait()
+        rows = pl.ds(pl.multiple_of(i * BLOCK, BLOCK), BLOCK)
         for j in range(groups):
+            at = pl.ds(i * BLOCK * SUB + j, BLOCK, stride=SUB)
             raw = dt_in[rows, j * LANES:(j + 1) * LANES].astype(F32)
-            dt_rows[pl.ds(i * 32 * SUB + j, 32, stride=SUB), :] = jnp.log2(1.0 + jnp.exp2(raw * LOG2E))
-        return 0
-
-    lax.fori_loop(0, tokens // 32, step_sizes, 0)
-
-    x_load.wait()
-
-    def lay_out(i, _):
-        rows = pl.ds(pl.multiple_of(i * 32, 32), 32)
-        for j in range(groups):
-            x_rows[pl.ds(i * 32 * SUB + j, 32, stride=SUB), :] = x_in[rows, j * LANES:(j + 1) * LANES].astype(F32)
-        return 0
-
-    lax.fori_loop(0, tokens // 32, lay_out, 0)
-    pl.when(jnp.logical_not(soon))(greet)
-
-    @pl.when(me < count - 1)
-    def _():
-        halo_copy.start()
-
+            dt_rows[at, :] = jnp.log2(1.0 + jnp.exp2(raw * LOG2E))
+            x_rows[at, :] = x_in[rows, j * LANES:(j + 1) * LANES].astype(F32)
+
+    lay_out(jnp.int32(0))
     w_load.wait()
     bias_load.wait()
     skip_load.wait()
@@ -183,23 +183,31 @@
         u_rows[tile(t), :] = dt_rows[tile(t), :] * inner
         y_rows[tile(t), :] = inner
 
-    total = zero
-    for t in range(HEAD):
-        total = total + dt_rows[tile(t), :]
-    head_total = total
-
-    def mix(i, carried):
+    def mix_block(i, carried):
         x0, x1, x2, total = carried
-        for k in range(MIX):
-            t = HEAD + i * MIX + k
+        for k in range(BLOCK):
+            t = i * BLOCK + k
             x3 = x_rows[tile(t), :]
             mix_token(t, (x0, x1, x2, x3))
             total = total + dt_rows[tile(t), :]
             x0, x1, x2 = x1, x2, x3
         return x0, x1, x2, total
 
-    window = tuple(x_rows[tile(t), :] for t in range(HEAD - 3, HEAD))
-    *_, total = lax.fori_loop(0, (tokens - HEAD) // MIX, mix, window + (total,))
+    def mix(i, carried):
+        lay_out(i + 1)
+        return mix_block(i, carried)
+
+    carried = lax.fori_loop(0, blocks - 1, mix, (zero,) * 4)
+    pl.when(jnp.logical_not(soon))(greet)
+
+    @pl.when(me < count - 1)
+    def _():
+        halo_copy.start()
+
+    *_, total = mix_block(jnp.int32(blocks - 1), carried)
+    head_total = zero
+    for t in range(HEAD):
+        head_total = head_total + dt_rows[tile(t), :]
 
     def advance(group, t, state):
         step = dt_rows[tile(t), :]
@@ -243,7 +251,7 @@
     size = (per + 1) * SUB
     mine = pl.ds(pl.multiple_of(place * size, SUB), size)
     sent = []
-    for step in (1, LINE - 1, 2, LINE - 2, 3, LINE - 3, LINE // 2):
+    for step in FAR_FIRST:
         know_place(step)
         target = (place + step) % LINE
         theirs = pl.ds(pl.multiple_of(target * size, SUB), size)
@@ -285,17 +293,6 @@
     c_load.wait()
     spread(c_in, c_splat, LN2)
     read_out(SHARES[0])
-    z_load.wait()
-
-    def gates(i, _):
-        rows = pl.ds(pl.multiple_of(i * 16, 16), 16)
-        for j in range(groups):
-            half = 0.5 * z_in[rows, j * LANES:(j + 1) * LANES].astype(F32)
-            gate[rows, j * LANES:(j + 1) * LANES] = half + half * jnp.tanh(half)
-        return 0
-
-    lax.fori_loop(0, tokens // 16, gates, 0)
-
     for copy in sent:
         copy.wait_recv()
     own_rate = [rates[tile(place * per + m), :] for m in range(per)]
@@ -324,6 +321,19 @@
             line_copy(step).start()
 
 
+    z_load.wait()
+
+    def gates(i, _):
+        rows = pl.ds(pl.multiple_of(i * 16, 16), 16)
+        for j in range(groups):
+            half = 0.5 * z_in[rows, j * LANES:(j + 1) * LANES].astype(F32)
+            gate[rows, j * LANES:(j + 1) * LANES] = half + half * jnp.tanh(half)
+        return 0
+
+    lax.fori_loop(0, tokens // 16, gates, 0)
+
+    read_out(SHARES[1])
+
     for m in range(per):
         carry[tile(m), :] = zero
     for step in range(lines - 1, 0, -1):
@@ -340,17 +350,20 @@
         for m in range(per):
             at = tile(other * per + m)
             starts_out[at, :] = starts_out[at, :] + spans[at, :] * carry[tile(m), :]
-    returned = []
     mine = tile(place * per, per)
-    for step in range(1, LINE):
+
+    def start_copy(step):
         target = (place + step) % LINE
-        copy = copy_to(starts_out.at[tile(target * per, per)], starts.at[mine], send3.at[step], recv3.at[step],
+        return copy_to(starts_out.at[tile(target * per, per)], starts.at[mine], send3.at[step], recv3.at[step],
                        line * LINE + target)
-        copy.start()
-        returned.append(copy)
+
+    returned = [start_copy(step) for step in range(1, LINE)]
+    for target in (0, 1, 2, 3, 7, 6, 5, 4):
+        @pl.when(place != target)
+        def _():
+            start_copy((target + LINE - place) % LINE).start()
     starts[mine, :] = starts_out[mine, :]
 
-    read_out(SHARES[1])
     read_out(SHARES[2])
 
     def start_terms(owners, t):
@@ -436,7 +449,7 @@
             rows(states * tokens),
             rows(3), rows(LINE * (per + 1)), rows(LINE * (per + 1)), rows(per + 1), rows(lines * (per + 1)), rows(per),
             rows(states), rows(states), rows(states),
-            pltpu.SemaphoreType.DMA((9,)), pltpu.SemaphoreType.REGULAR((LINE,)),
+            pltpu.SemaphoreType.DMA((7,)), pltpu.SemaphoreType.DMA((tokens // BLOCK,)), pltpu.SemaphoreType.DMA((tokens // BLOCK,)), pltpu.SemaphoreType.REGULAR((LINE,)),
             pltpu.SemaphoreType.REGULAR((lines,)), pltpu.SemaphoreType.DMA((2,)),
             pltpu.SemaphoreType.DMA((LINE,)), pltpu.SemaphoreType.DMA((LINE,)),
             pltpu.SemaphoreType.DMA((lines,)), pltpu.SemaphoreType.DMA((lines,)),

time: 26.8 us -> 25.9 us (0.966)
  Pallas kernels: 25.8 us -> 25 us
    pallas_call x1, Pallas kernels: 25.8 us -> 25 us  [body(): pl.pallas_call(functools.partial(kernel, lines), out_shape=pltpu.VMEM((to...]
where the time goes in v3:
time: 25.9 us; the launch traced here: 25.8 us
  Pallas kernels  25 us (97%)
  local copies, waits for them, and re-layouts  0.8 us (3%)
    pallas_call x1, Pallas kernels, body(): pl.pallas_call(functools.partial(kernel, lines), out_shape=pltpu.VMEM((to...  25 us
    unnamed x1, local copies, waits for them, and re-layouts  0.8 us

profile of v3, /device:TPU:448, one launch (start us, length us, event | category | flops | bytes accessed | tf_op | source)
XLA Modules:
  0.0 25.8 jit_solution(3748510198854641436)
XLA Ops:
  0.0 25.0 %shard_map.91 = bf16[256,1024]{1,0:T(8,128)(2,1)S(1)} custom-call(bf16[256,1024]{1,0:T(8,128)(2,1)} %x_hbm.1, bf16[256,1024]{1,0:T(8,128)(2,1)} %z_hbm.1, bf16[256,1024]{1,0:T(8,128)(2,1)} %dt_hbm.1, bf16[16,256]{1,0:T(8,128)(2,1)} %bitcast.4, bf16[16,256]{1,0:T(8,128)(2,1)} %bitcast.5, f32[4,1024]{1,0:T(4,128)} %w_hbm.1, f32[8,128]{1,0:T(8,128)} %bitcast.6, ...), custom_call_target="tpu_custom_call" | custom-call | tf_op jit(solution)/shard_map/pallas_call | solution.py:460
  25.0 0.8 %copy.11 = bf16[256,1024]{1,0:T(8,128)(2,1)} copy(bf16[256,1024]{1,0:T(8,128)(2,1)S(1)} %shard_map.91) | data formatting | bytes 1048576

commit v4 on v3

--- a/solution.py
+++ b/solution.py
@@ -13,7 +13,7 @@
 SUB = 8
 LINE = 8
 HEAD = 4
-LINE_RANKS = (0, 1, 4, 5, 2, 3, 6, 7)
+LINE_RANKS = (0, 1, 2, 3, 4, 5, 6, 7)
 FAR_FIRST = (4, 3, 5, 2, 6, 1, 7)
 BLOCK = 32
 SCAN = 42

time: 25.9 us -> 25.3 us (0.977)
  Pallas kernels: 25 us -> 24.3 us
    pallas_call x1, Pallas kernels: 25 us -> 24.3 us  [body(): pl.pallas_call(functools.partial(kernel, lines), out_shape=pltpu.VMEM((to...]
where the time goes in v4:
time: 25.3 us; the launch traced here: 25.1 us
  Pallas kernels  24.3 us (96%)
  local copies, waits for them, and re-layouts  0.8 us (3%)
    pallas_call x1, Pallas kernels, body(): pl.pallas_call(functools.partial(kernel, lines), out_shape=pltpu.VMEM((to...  24.3 us
    unnamed x1, local copies, waits for them, and re-layouts  0.8 us

profile of v4, /device:TPU:448, one launch (start us, length us, event | category | flops | bytes accessed | tf_op | source)
XLA Modules:
  0.0 25.1 jit_solution(17739674500274540097)
XLA Ops:
  0.0 24.3 %shard_map.91 = bf16[256,1024]{1,0:T(8,128)(2,1)S(1)} custom-call(bf16[256,1024]{1,0:T(8,128)(2,1)} %x_hbm.1, bf16[256,1024]{1,0:T(8,128)(2,1)} %z_hbm.1, bf16[256,1024]{1,0:T(8,128)(2,1)} %dt_hbm.1, bf16[16,256]{1,0:T(8,128)(2,1)} %bitcast.4, bf16[16,256]{1,0:T(8,128)(2,1)} %bitcast.5, f32[4,1024]{1,0:T(4,128)} %w_hbm.1, f32[8,128]{1,0:T(8,128)} %bitcast.6, ...), custom_call_target="tpu_custom_call" | custom-call | tf_op jit(solution)/shard_map/pallas_call | solution.py:460
  24.3 0.8 %copy.11 = bf16[256,1024]{1,0:T(8,128)(2,1)} copy(bf16[256,1024]{1,0:T(8,128)(2,1)S(1)} %shard_map.91) | data formatting | bytes 1048576

commit v5 on v4

--- a/solution.py
+++ b/solution.py
@@ -19,7 +19,7 @@
 SCAN = 42
 LOG2E = 1.4426950408889634
 LN2 = 0.6931471805599453
-SHARES = ((0, 1, 2, 3), (4, 5, 6, 7), (8, 9, 10, 11, 12, 13, 14, 15))
+SHARES = (((0, 1, 2, 3), (4, 5)), ((6, 7, 8, 9), (10, 11)), ((12, 13, 14, 15),))
 
 
 def tile(index, count=1):
@@ -292,7 +292,8 @@
 
     c_load.wait()
     spread(c_in, c_splat, LN2)
-    read_out(SHARES[0])
+    for share in SHARES[0]:
+        read_out(share)
     for copy in sent:
         copy.wait_recv()
     own_rate = [rates[tile(place * per + m), :] for m in range(per)]
@@ -332,7 +333,8 @@
 
     lax.fori_loop(0, tokens // 16, gates, 0)
 
-    read_out(SHARES[1])
+    for share in SHARES[1]:
+        read_out(share)
 
     for m in range(per):
         carry[tile(m), :] = zero
@@ -364,7 +366,8 @@
             start_copy((target + LINE - place) % LINE).start()
     starts[mine, :] = starts_out[mine, :]
 
-    read_out(SHARES[2])
+    for share in SHARES[2]:
+        read_out(share)
 
     def start_terms(owners, t):
         terms = []

time: 25.3 us -> 25.3 us (level)
  no operation moved by 1% of the time
where the time goes in v5:
time: 25.3 us; the launch traced here: 25.1 us
  Pallas kernels  24.3 us (96%)
  local copies, waits for them, and re-layouts  0.8 us (3%)
    pallas_call x1, Pallas kernels, body(): pl.pallas_call(functools.partial(kernel, lines), out_shape=pltpu.VMEM((to...  24.3 us
    unnamed x1, local copies, waits for them, and re-layouts  0.8 us

profile of v5, /device:TPU:448, one launch (start us, length us, event | category | flops | bytes accessed | tf_op | source)
XLA Modules:
  0.0 25.1 jit_solution(9816461233212912778)
XLA Ops:
  0.0 24.3 %shard_map.91 = bf16[256,1024]{1,0:T(8,128)(2,1)S(1)} custom-call(bf16[256,1024]{1,0:T(8,128)(2,1)} %x_hbm.1, bf16[256,1024]{1,0:T(8,128)(2,1)} %z_hbm.1, bf16[256,1024]{1,0:T(8,128)(2,1)} %dt_hbm.1, bf16[16,256]{1,0:T(8,128)(2,1)} %bitcast.4, bf16[16,256]{1,0:T(8,128)(2,1)} %bitcast.5, f32[4,1024]{1,0:T(4,128)} %w_hbm.1, f32[8,128]{1,0:T(8,128)} %bitcast.6, ...), custom_call_target="tpu_custom_call" | custom-call | tf_op jit(solution)/shard_map/pallas_call | solution.py:463
  24.3 0.8 %copy.11 = bf16[256,1024]{1,0:T(8,128)(2,1)} copy(bf16[256,1024]{1,0:T(8,128)(2,1)S(1)} %shard_map.91) | data formatting | bytes 1048576
